TPU v7x, 512 devices: a whole 4x4x16 slice. The times are simulated.
512 devices in a mesh: dp: 64 (over z_lo, y, core), fsdp: 8 (over x, z_hi).
Axes of the slice: x: 4, y: 4, z: 16 (z_hi: 2, z_lo: 8; z = z_hi * 8 + z_lo), core: 2. Of those that a mesh axis runs over, the one named last changes fastest.
Arguments:
- tokens: bfloat16 [512, 16384], P('dp', 'fsdp'), may hold values from -6 to 6
- route_plan: int32 [4], replicated, may hold values from -1 to 3, as said below
- block_tokens: int32 [4], replicated, may hold values from 1 to 128
- gate_up: bfloat16 [16384, 2, 26624], P('fsdp', None, 'dp'), may hold values from -0.046875 to 0.046875
- down_proj: bfloat16 [26624, 16384], P('dp', 'fsdp'), may hold values from -0.0390625 to 0.0390625
Outputs:
- layer_output: bfloat16 [512, 16384], P('dp', 'fsdp')
Inputs may be any that keep to these rules, and one draw needn't show every extreme that they name: route_plan[b] is -1 for an empty source block; no two source blocks name the same destination block.
All inputs are finite; a program needn't handle non-finite values.
Results may differ from a plain program's by a relative error of at most 0.0049.
Values may be sent and summed in bfloat16 or wider, within the bound.
No kernel may reach another device: no remote copies, remote signals or barrier semaphores. Data moves between devices by JAX's collectives and lax.ppermute only.
A program may use at most 64 MiB of HBM per device.

v0:
```python
import functools

import jax
import jax.numpy as jnp
from jax import lax
from jax.experimental import pallas as pl
from jax.experimental.pallas import tpu as pltpu
from jax.sharding import Mesh
from jax.sharding import PartitionSpec as P

BLK = 128
HALF = 64
ZL, YY, CC, XX, ZH = 8, 4, 2, 4, 2
WIDE = 256
SIZES = (2, 3, 4, 5, 6, 8)
BF16, F32 = jnp.bfloat16, jnp.float32


def halves_of(plan, lives):
    slot = jnp.int32(0)
    for h in range(ZL):
        block, part = h // 2, h % 2
        live = (plan(block) >= 0) & (lives(block) > HALF * part)
        yield h, block, part, live, slot
        slot = slot + live.astype(jnp.int32)


def pack_kernel(slots, plan_ref, lives_ref, place_ref, rows_ref, out_ref):
    row = lax.broadcasted_iota(jnp.int32, rows_ref.shape[1:], 0) + place_ref[0]
    count = jnp.int32(0)
    for h, block, part, live, slot in halves_of(lambda b: plan_ref[b], lambda b: lives_ref[b]):
        count = slot + live.astype(jnp.int32)

        @pl.when(live)
        def _():
            kept = row + HALF * part < lives_ref[block]
            rows = jnp.where(kept, rows_ref[h].astype(F32), 0.0).astype(BF16)
            for copy in range(YY):
                out_ref[copy, slot] = rows

    for s in range(slots):

        @pl.when(s >= count)
        def _():
            for copy in range(YY):
                out_ref[copy, s] = jnp.zeros(out_ref.shape[2:], BF16)


def place_kernel(plan_ref, lives_ref, parts_ref, out_ref):
    out_ref[...] = jnp.zeros(out_ref.shape, BF16)
    for h, block, part, live, slot in halves_of(lambda b: plan_ref[b], lambda b: lives_ref[b]):

        @pl.when(live)
        def _():
            total = parts_ref[0, slot].astype(F32)
            for k in range(1, YY):
                total = total + parts_ref[k, slot].astype(F32)
            out_ref[2 * plan_ref[block] + part] = total.astype(BF16)


def project_kernel(rows_ref, own_ref, other_ref, out_ref, weights, arrived):
    share = own_ref.shape[1]
    copies = []
    for k in range(4):
        source = (own_ref, other_ref)[k % 2]
        copies.append(
            pltpu.make_async_copy(source.at[k // 2], weights.at[pl.ds(k * share, share)], arrived.at[k])
        )
        copies[-1].start()
    rows = rows_ref[...]
    have = 0
    for low in range(0, 4 * share, WIDE):
        high = min(low + WIDE, 4 * share)
        while have < high:
            copies[have // share].wait()
            have += share
        out_ref[:, low:high] = lax.dot_general(
            rows, weights[low:high], (((1,), (1,)), ((), ())), preferred_element_type=F32
        )


def project(rows, own, other):
    count, features = rows.shape
    columns = 4 * own.shape[1]
    return pl.pallas_call(
        project_kernel,
        out_shape=jax.ShapeDtypeStruct((count, columns), F32),
        in_specs=[pl.BlockSpec(memory_space=pltpu.VMEM)] + [pl.BlockSpec(memory_space=pl.ANY)] * 2,
        out_specs=pl.BlockSpec(memory_space=pltpu.VMEM),
        scratch_shapes=[pltpu.VMEM((columns, features), BF16), pltpu.SemaphoreType.DMA((4,))],
        compiler_params=pltpu.CompilerParams(vmem_limit_bytes=32 << 20),
        cost_estimate=pl.CostEstimate(
            flops=2 * count * columns * features, bytes_accessed=2 * columns * features, transcendentals=0
        ),
    )(rows, own, other)


def local_call(kernel, scalars, shape):
    return pl.pallas_call(
        kernel,
        out_shape=jax.ShapeDtypeStruct(shape, BF16),
        in_specs=[pl.BlockSpec(memory_space=pltpu.SMEM)] * scalars + [pl.BlockSpec(memory_space=pltpu.VMEM)],
        out_specs=pl.BlockSpec(memory_space=pltpu.VMEM),
        compiler_params=pltpu.CompilerParams(vmem_limit_bytes=16 << 20),
    )


def exchange(array, axis):
    return lax.all_to_all(array, axis, 0, 0, tiled=False)


def swap(array, axis):
    return lax.ppermute(array, axis, [(0, 1), (1, 0)])


def spread(array, copies):
    return jnp.broadcast_to(array[None], (copies,) + array.shape)


def block_rows(slots, gathered, plan, lives, own, other, down):
    features, hidden = own.shape[2], 2 * down[0].shape[0]
    per = slots * 8
    place = (lax.axis_index("y") * 16 + lax.axis_index("c") * 8).reshape(1)
    packed = local_call(functools.partial(pack_kernel, slots), 3, (YY, slots, 8, features))(plan, lives, place, gathered)
    rows = exchange(packed.reshape(YY, per, features), "y").reshape(YY * per, features)

    partial = project(rows, own, other)
    along_x = jnp.sum(exchange(partial.reshape(XX, per, 2 * hidden), "x"), axis=0)
    across = swap(along_x.astype(BF16), "zh").astype(F32)
    down = jnp.concatenate(down, axis=0)
    summed = along_x + across
    act = (jax.nn.silu(summed[:, :hidden]) * summed[:, hidden:]).astype(BF16)
    act = exchange(spread(act, XX), "x").reshape(XX * per, hidden)

    ours = jnp.dot(act, down, preferred_element_type=F32).astype(BF16)
    parts = exchange(ours.reshape(YY, per, -1), "y").reshape(YY, slots, 8, -1)
    return local_call(place_kernel, 2, (ZL, 8, down.shape[1]))(plan, lives, parts)


def body(tokens, plan, lives, weights, down):
    gathered = exchange(spread(tokens, ZL), "zl")
    weights = weights.transpose(1, 2, 0)
    other = swap(weights, "c")
    down = (down, swap(down, "c"))
    if len(SIZES) == 1:
        placed = block_rows(SIZES[0], gathered, plan, lives, weights, other, down)
    else:
        count = jnp.sum((plan >= 0) * (1 + (lives > HALF)))
        which = sum((count > n).astype(jnp.int32) for n in SIZES[:-1])
        placed = lax.switch(
            which, [functools.partial(block_rows, n) for n in SIZES], gathered, plan, lives, weights, other, down
        )
    sums = exchange(placed, "zl")
    total = sums[0].astype(F32)
    for k in range(1, ZL):
        total = total + sums[k].astype(F32)
    return total.astype(BF16)


def solution(mesh):
    fine = Mesh(mesh.devices.reshape(ZL, YY, CC, XX, ZH), ("zl", "y", "c", "x", "zh"))
    dp, fsdp = ("zl", "y", "c"), ("x", "zh")
    return jax.shard_map(
        body,
        mesh=fine,
        in_specs=(P(dp, fsdp), P(), P(), P(fsdp, None, dp), P(dp, fsdp)),
        out_specs=P(dp, fsdp),
        check_vma=False,
    )
```

profile of v0, /device:TPU:32, one launch (start us, length us, event | category | flops | bytes accessed | tf_op | source)
XLA Modules:
  0.0 133.0 jit_solution(8246675810088112666)
XLA Ops:
  0.0 1.9 %collective-permute-start.6 = (bf16[2,416,2048]{2,1,0:T(8,128)(2,1)}, bf16[2,416,2048]{2,1,0:T(8,128)(2,1)}, u32[]{:S(2)}, u32[]{:S(2)}) collective-permute-start(bf16[2,416,2048]{2,1,0:T(8,128)(2,1)} %bitcast.75), channel_id=1, source_target_pairs={{0,8},{8,0},{1,9},{9,1},{2,10},{10,2},{3,11},{11,3},{4,12},{12,4},... | collective-permute-start | bytes 10223624 | tf_op jit(solution)/shard_map/ppermute | solution.py:113
  1.9 2.4 %collective-permute-start.7 = (bf16[416,2048]{1,0:T(8,128)(2,1)}, bf16[416,2048]{1,0:T(8,128)(2,1)}, u32[]{:S(2)}, u32[]{:S(2)}) collective-permute-start(bf16[416,2048]{1,0:T(8,128)(2,1)} %param.15), channel_id=1, source_target_pairs={{0,8},{8,0},{1,9},{9,1},{2,10},{10,2},{3,11},{11,3},{4,12},{12,4},... | collective-permute-start | bytes 5111816 | tf_op jit(solution)/shard_map/ppermute | solution.py:113
  4.3 1.5 %broadcast_in_dim.22 = bf16[8,8,2048]{2,1,0:T(8,128)(2,1)} broadcast(bf16[8,2048]{1,0:T(8,128)(2,1)} %param.11), dimensions={1,2} | broadcast | bytes 294912 | tf_op jit(solution)/shard_map/broadcast_in_dim | solution.py:117
  5.8 12.6 %all-to-all-start.24 = ((bf16[8,8,2048]{2,1,0:T(8,128)(2,1)}), bf16[8,8,2048]{2,1,0:T(8,128)(2,1)}, u32[]{:S(2)}, u32[]{:S(2)}) async-start(bf16[8,8,2048]{2,1,0:T(8,128)(2,1)} %broadcast_in_dim.22), calls=%async_computation.24 | async-start | bytes 524288 | tf_op jit(solution)/shard_map/all_to_all | solution.py:109
  18.4 1.3 fusion.55
  23.0 12.0 %all-to-all-done.24 = bf16[8,8,2048]{2,1,0:T(8,128)(2,1)} async-done(((bf16[8,8,2048]{2,1,0:T(8,128)(2,1)}), bf16[8,8,2048]{2,1,0:T(8,128)(2,1)}, u32[]{:S(2)}, u32[]{:S(2)}) %all-to-all-start.24) | async-done | bytes 262176 | tf_op jit(solution)/shard_map/all_to_all | solution.py:109
  35.0 0.0 collective-permute-done.7
  35.0 0.0 collective-permute-done.6
  35.0 78.0 %conditional.1 = (bf16[8,8,2048]{2,1,0:T(8,128)(2,1)S(1)}) conditional(s32[]{:T(128)} %clamp.3, (s32[4]{0:T(128)}, s32[4]{0:T(128)}, bf16[8,8,2048]{2,1,0:T(8,128)(2,1)}, bf16[2,416,2048]{2,1,0:T(8,128)(2,1)}, bf16[2,416,2048]{2,1,0:T(8,128)(2,1)}, /*index=5*/bf16[416,2048]{1,0:T(8,128)(2,1)}, ...), branch_computations={%region_1.3_spmd, %region_3.5_spmd, %region_5.7_spmd, %region_7.9_... | conditional | flops 2625544192 | bytes 46350728 | solution.py:150
  35.0 1.1 branch_3_fun.3
  36.1 13.1 %all_to_all.118 = bf16[4,40,2048]{2,1,0:T(8,128)(2,1)S(1)} all-to-all(bf16[4,40,2048]{2,1,0:T(8,128)(2,1)S(1)} %bitcast.62), channel_id=1, replica_groups=mesh['zl'=8,'y'=4,'c'=2,'x'=4,'zh'=2] {'y'}, dimensions={0} | all-to-all | bytes 1310720 | tf_op jit(solution)/shard_map/cond/branch_3_fun/all_to_all | solution.py:109
  49.1 4.8 %branch_3_fun.4 = f32[160,1664]{1,0:T(8,128)S(1)} custom-call(bf16[160,2048]{1,0:T(8,128)(2,1)S(1)} %bitcast.61, bf16[2,416,2048]{2,1,0:T(8,128)(2,1)} %get-tuple-element.120.own_ref, bf16[2,416,2048]{2,1,0:T(8,128)(2,1)} %get-tuple-element.121.other_ref), custom_call_target="tpu_custom_call" | custom-call | flops 1090519040 | bytes 6815744 | tf_op jit(solution)/shard_map/cond/branch_3_fun/pallas_call | solution.py:85
  53.9 0.0 copy-start.16
  53.9 15.2 %all_to_all.119 = f32[4,40,1664]{2,1,0:T(8,128)S(1)} all-to-all(f32[4,40,1664]{2,1,0:T(8,128)S(1)} %bitcast.53), channel_id=1, replica_groups=mesh['zl'=8,'y'=4,'c'=2,'x'=4,'zh'=2] {'x'}, dimensions={0} | all-to-all | bytes 2129920 | tf_op jit(solution)/shard_map/cond/branch_3_fun/all_to_all | solution.py:109
  69.1 0.1 reduce_sum.59
  69.2 8.2 %collective-permute-start.3 = (bf16[40,1664]{1,0:T(8,128)(2,1)S(1)}, bf16[40,1664]{1,0:T(8,128)(2,1)S(1)}, u32[]{:S(2)}, u32[]{:S(2)}) collective-permute-start(bf16[40,1664]{1,0:T(8,128)(2,1)S(1)} %convert_element_type.103), channel_id=1, source_target_pairs={{0,1},{1,0},{2,3},{3,2},{4,5},{5,4},{6,7},{7,6},{8,9},{9,8},{10,11... | collective-permute-start | bytes 399368 | tf_op jit(solution)/shard_map/cond/branch_3_fun/ppermute | solution.py:113
  77.5 11.4 %collective-permute-done.3 = bf16[40,1664]{1,0:T(8,128)(2,1)S(1)} collective-permute-done((bf16[40,1664]{1,0:T(8,128)(2,1)S(1)}, bf16[40,1664]{1,0:T(8,128)(2,1)S(1)}, u32[]{:S(2)}, u32[]{:S(2)}) %collective-permute-start.3) | collective-permute-done | bytes 133152 | tf_op jit(solution)/shard_map/cond/branch_3_fun/ppermute | solution.py:113
  88.9 0.1 fusion.34
  89.1 9.2 %all_to_all.120 = bf16[4,40,832]{2,1,0:T(8,128)(2,1)S(1)} all-to-all(bf16[4,40,832]{2,1,0:T(8,128)(2,1)S(1)} %broadcast_in_dim.14), channel_id=1, replica_groups=mesh['zl'=8,'y'=4,'c'=2,'x'=4,'zh'=2] {'x'}, dimensions={0} | all-to-all | bytes 532480 | tf_op jit(solution)/shard_map/cond/branch_3_fun/all_to_all | solution.py:109
  98.2 2.4 %fusion.31 = bf16[160,2048]{1,0:T(8,128)(2,1)S(1)} fusion(bf16[160,832]{1,0:T(8,128)(2,1)S(1)} %bitcast.89, bf16[416,2048]{1,0:T(8,128)(2,1)} %get-tuple-element.123, bf16[416,2048]{1,0:T(8,128)(2,1)S(1)} %copy-done.16), kind=kOutput, calls=%fused_computation.31 | convolution fusion | flops 552402944 | bytes 4329472 | tf_op jit(solution)/shard_map/cond/branch_3_fun/dot_general | solution.py:135
  100.6 11.2 %all_to_all.121 = bf16[4,40,2048]{2,1,0:T(8,128)(2,1)S(1)} all-to-all(bf16[4,40,2048]{2,1,0:T(8,128)(2,1)S(1)} %bitcast.84), channel_id=1, replica_groups=mesh['zl'=8,'y'=4,'c'=2,'x'=4,'zh'=2] {'y'}, dimensions={0} | all-to-all | bytes 1310720 | tf_op jit(solution)/shard_map/cond/branch_3_fun/all_to_all | solution.py:109
  111.8 0.7 branch_3_fun.5
  113.0 19.4 %all_to_all.130 = bf16[8,8,2048]{2,1,0:T(8,128)(2,1)S(1)} all-to-all(bf16[8,8,2048]{2,1,0:T(8,128)(2,1)S(1)} %get-tuple-element.138), channel_id=1, replica_groups=mesh['zl'=8,'y'=4,'c'=2,'x'=4,'zh'=2] {'zl'}, dimensions={0} | all-to-all | bytes 524288 | tf_op jit(solution)/shard_map/all_to_all | solution.py:109
  132.4 0.7 fusion.54
  (8 shorter events, 0.1 us)
Async XLA Ops:
  0.0 35.0 %collective-permute-start.6 = (bf16[2,416,2048]{2,1,0:T(8,128)(2,1)}, bf16[2,416,2048]{2,1,0:T(8,128)(2,1)}, u32[]{:S(2)}, u32[]{:S(2)}) collective-permute-start(bf16[2,416,2048]{2,1,0:T(8,128)(2,1)} %bitcast.75), channel_id=1, source_target_pairs={{0,8},{8,0},{1,9},{9,1},{2,10},{10,2},{3,11},{11,3},{4,12},{12,4},... | collective-permute-start | bytes 10223624 | tf_op jit(solution)/shard_map/ppermute | solution.py:113
  1.9 33.0 %collective-permute-start.7 = (bf16[416,2048]{1,0:T(8,128)(2,1)}, bf16[416,2048]{1,0:T(8,128)(2,1)}, u32[]{:S(2)}, u32[]{:S(2)}) collective-permute-start(bf16[416,2048]{1,0:T(8,128)(2,1)} %param.15), channel_id=1, source_target_pairs={{0,8},{8,0},{1,9},{9,1},{2,10},{10,2},{3,11},{11,3},{4,12},{12,4},... | collective-permute-start | bytes 5111816 | tf_op jit(solution)/shard_map/ppermute | solution.py:113
  5.8 29.2 %all-to-all-start.24 = ((bf16[8,8,2048]{2,1,0:T(8,128)(2,1)}), bf16[8,8,2048]{2,1,0:T(8,128)(2,1)}, u32[]{:S(2)}, u32[]{:S(2)}) async-start(bf16[8,8,2048]{2,1,0:T(8,128)(2,1)} %broadcast_in_dim.22), calls=%async_computation.24 | async-start | bytes 524288 | tf_op jit(solution)/shard_map/all_to_all | solution.py:109
  53.9 44.3 %copy-start.16 = (bf16[416,2048]{1,0:T(8,128)(2,1)S(1)}, bf16[416,2048]{1,0:T(8,128)(2,1)}, u32[]{:S(2)}) copy-start(bf16[416,2048]{1,0:T(8,128)(2,1)} %get-tuple-element.122) | copy-start | bytes 5111812 | tf_op jit(solution)/shard_map/cond
  69.2 19.7 %collective-permute-start.3 = (bf16[40,1664]{1,0:T(8,128)(2,1)S(1)}, bf16[40,1664]{1,0:T(8,128)(2,1)S(1)}, u32[]{:S(2)}, u32[]{:S(2)}) collective-permute-start(bf16[40,1664]{1,0:T(8,128)(2,1)S(1)} %convert_element_type.103), channel_id=1, source_target_pairs={{0,1},{1,0},{2,3},{3,2},{4,5},{5,4},{6,7},{7,6},{8,9},{9,8},{10,11... | collective-permute-start | bytes 399368 | tf_op jit(solution)/shard_map/cond/branch_3_fun/ppermute | solution.py:113
  98.2 13.6 %copy-start.4 = (s32[4]{0:T(128)S(1)}, s32[4]{0:T(128)}, u32[]{:S(2)}) copy-start(s32[4]{0:T(128)} %get-tuple-element.117.plan_ref) | copy-start | bytes 52 | tf_op jit(solution)/shard_map/cond
  98.2 13.6 %copy-start.10 = (s32[4]{0:T(128)S(1)}, s32[4]{0:T(128)}, u32[]{:S(2)}) copy-start(s32[4]{0:T(128)} %get-tuple-element.118.lives_ref) | copy-start | bytes 52 | tf_op jit(solution)/shard_map/cond
where the time goes:
time: 134 us; the launch traced here: 133 us
  blocking collectives  68 us (51%)
  starting transfers between devices  25.2 us (19%)
  waiting for transfers between devices  23.4 us (17%)
  Pallas kernels  6.58 us (5%)
  between operations  3.27 us (2%)
  matrix products  2.37 us (2%)
  other arithmetic  2.19 us (2%)
  local copies, waits for them, and re-layouts  1.51 us (1%)
    all_to_all x5, blocking collectives, exchange(): return lax.all_to_all(array, axis, 0, 0, tiled=False)  68 us
    all_to_all x1, starting transfers between devices, exchange(): return lax.all_to_all(array, axis, 0, 0, tiled=False)  12.6 us
    ppermute x3, starting transfers between devices, swap(): return lax.ppermute(array, axis, [(0, 1), (1, 0)])  12.5 us
    all_to_all x1, waiting for transfers between devices, exchange(): return lax.all_to_all(array, axis, 0, 0, tiled=False)  12 us
    ppermute x3, waiting for transfers between devices, swap(): return lax.ppermute(array, axis, [(0, 1), (1, 0)])  11.4 us
    pallas_call x1, Pallas kernels, project(): pl.pallas_call(project_kernel, out_shape=jax.ShapeDtypeStruct((count, col...  4.76 us
  transfers between devices with their start and end apart: 4, of which 2 were waited for; matrix products, arithmetic and copies ran while one was open for 2% of the time, Pallas kernels for 0%

commit v1 on v0

--- a/solution.py
+++ b/solution.py
@@ -11,6 +11,7 @@
 BLK = 128
 HALF = 64
 ZL, YY, CC, XX, ZH = 8, 4, 2, 4, 2
+HIDE = 40_000_000_000
 WIDE = 256
 SIZES = (2, 3, 4, 5, 6, 8)
 BF16, F32 = jnp.bfloat16, jnp.float32
@@ -23,6 +24,27 @@
         live = (plan(block) >= 0) & (lives(block) > HALF * part)
         yield h, block, part, live, slot
         slot = slot + live.astype(jnp.int32)
+
+
+def size_kernel(plan_ref, lives_ref, out_ref):
+    count = jnp.int32(0)
+    for h, block, part, live, slot in halves_of(lambda b: plan_ref[b], lambda b: lives_ref[b]):
+        count = slot + live.astype(jnp.int32)
+    which = jnp.int32(0)
+    for n in SIZES[:-1]:
+        which = which + (count > n).astype(jnp.int32)
+    out_ref[0] = which
+
+
+def pick_size(plan, lives):
+    return pl.pallas_call(
+        size_kernel,
+        out_shape=jax.ShapeDtypeStruct((1,), jnp.int32),
+        in_specs=[pl.BlockSpec(memory_space=pltpu.SMEM)] * 2,
+        out_specs=pl.BlockSpec(memory_space=pltpu.SMEM),
+        compiler_params=pltpu.CompilerParams(vmem_limit_bytes=1 << 20),
+        cost_estimate=pl.CostEstimate(flops=HIDE, bytes_accessed=0, transcendentals=0),
+    )(plan, lives)[0]
 
 
 def pack_kernel(slots, plan_ref, lives_ref, place_ref, rows_ref, out_ref):
@@ -142,14 +164,11 @@
     weights = weights.transpose(1, 2, 0)
     other = swap(weights, "c")
     down = (down, swap(down, "c"))
-    if len(SIZES) == 1:
-        placed = block_rows(SIZES[0], gathered, plan, lives, weights, other, down)
-    else:
-        count = jnp.sum((plan >= 0) * (1 + (lives > HALF)))
-        which = sum((count > n).astype(jnp.int32) for n in SIZES[:-1])
-        placed = lax.switch(
-            which, [functools.partial(block_rows, n) for n in SIZES], gathered, plan, lives, weights, other, down
-        )
+    placed = lax.switch(
+        pick_size(plan, lives),
+        [functools.partial(block_rows, n) for n in SIZES],
+        gathered, plan, lives, weights, other, down,
+    )
     sums = exchange(placed, "zl")
     total = sums[0].astype(F32)
     for k in range(1, ZL):

time: 134 us -> 114 us (0.85)
  blocking collectives: 68 us -> 57.5 us
  waiting for transfers between devices: 23.4 us -> 16.8 us
  between operations: 3.27 us -> 0.73 us
  other arithmetic: 2.19 us -> 0.78 us
    all_to_all x5, blocking collectives: 68 us -> 57.5 us  [exchange(): return lax.all_to_all(array, axis, 0, 0, tiled=False)]
    ppermute x3, waiting for transfers between devices: 11.4 us -> 6.96 us  [swap(): return lax.ppermute(array, axis, [(0, 1), (1, 0)])]
    all_to_all x1, waiting for transfers between devices: 12 us -> 9.88 us  [exchange(): return lax.all_to_all(array, axis, 0, 0, tiled=False)]
  transfers between devices with their start and end apart: 4 -> 4, of which waited for: 2 -> 2; matrix products, arithmetic and copies ran while one was open for 2% -> 0% of each run, Pallas kernels for 0% -> 1%
where the time goes in v1:
time: 114 us; the launch traced here: 113 us
  blocking collectives  57.5 us (50%)
  starting transfers between devices  25.4 us (22%)
  waiting for transfers between devices  16.8 us (15%)
  Pallas kernels  7.17 us (6%)
  matrix products  2.74 us (2%)
  local copies, waits for them, and re-layouts  1.53 us (1%)
    all_to_all x5, blocking collectives, exchange(): return lax.all_to_all(array, axis, 0, 0, tiled=False)  57.5 us
    ppermute x3, starting transfers between devices, swap(): return lax.ppermute(array, axis, [(0, 1), (1, 0)])  12.8 us
    all_to_all x1, starting transfers between devices, exchange(): return lax.all_to_all(array, axis, 0, 0, tiled=False)  12.6 us
    all_to_all x1, waiting for transfers between devices, exchange(): return lax.all_to_all(array, axis, 0, 0, tiled=False)  9.88 us
    ppermute x3, waiting for transfers between devices, swap(): return lax.ppermute(array, axis, [(0, 1), (1, 0)])  6.96 us
    pallas_call x1, Pallas kernels, project(): pl.pallas_call(project_kernel, out_shape=jax.ShapeDtypeStruct((count, col...  4.22 us
    dot_general x1, matrix products, block_rows(): ours = jnp.dot(act, down, preferred_element_type=F32).astype(BF16)  2.74 us
  transfers between devices with their start and end apart: 4, of which 2 were waited for; matrix products, arithmetic and copies ran while one was open for 0% of the time, Pallas kernels for 1%

profile of v1, /device:TPU:32, one launch (start us, length us, event | category | flops | bytes accessed | tf_op | source)
XLA Modules:
  0.0 113.0 jit_solution(5738799895478989919)
XLA Ops:
  0.0 1.5 %broadcast_in_dim.22 = bf16[8,8,2048]{2,1,0:T(8,128)(2,1)} broadcast(bf16[8,2048]{1,0:T(8,128)(2,1)} %param.11), dimensions={1,2} | broadcast | bytes 294912 | tf_op jit(solution)/shard_map/broadcast_in_dim | solution.py:139
  1.5 12.6 %all-to-all-start.24 = ((bf16[8,8,2048]{2,1,0:T(8,128)(2,1)}), bf16[8,8,2048]{2,1,0:T(8,128)(2,1)}, u32[]{:S(2)}, u32[]{:S(2)}) async-start(bf16[8,8,2048]{2,1,0:T(8,128)(2,1)} %broadcast_in_dim.22), calls=%async_computation.24 | async-start | bytes 524288 | tf_op jit(solution)/shard_map/all_to_all | solution.py:131
  14.1 1.9 %collective-permute-start.7 = (bf16[416,2048]{1,0:T(8,128)(2,1)}, bf16[416,2048]{1,0:T(8,128)(2,1)}, u32[]{:S(2)}, u32[]{:S(2)}) collective-permute-start(bf16[416,2048]{1,0:T(8,128)(2,1)} %param.15), channel_id=1, source_target_pairs={{0,8},{8,0},{1,9},{9,1},{2,10},{10,2},{3,11},{11,3},{4,12},{12,4},... | collective-permute-start | bytes 5111816 | tf_op jit(solution)/shard_map/ppermute | solution.py:135
  16.1 0.0 copy-start
  16.1 0.0 copy-start.1
  16.1 0.0 copy-start.2
  16.1 2.7 %collective-permute-start.6 = (bf16[2,416,2048]{2,1,0:T(8,128)(2,1)}, bf16[2,416,2048]{2,1,0:T(8,128)(2,1)}, u32[]{:S(2)}, u32[]{:S(2)}) collective-permute-start(bf16[2,416,2048]{2,1,0:T(8,128)(2,1)} %bitcast.76), channel_id=1, source_target_pairs={{0,8},{8,0},{1,9},{9,1},{2,10},{10,2},{3,11},{11,3},{4,12},{12,4},... | collective-permute-start | bytes 10223624 | tf_op jit(solution)/shard_map/ppermute | solution.py:135
  18.8 1.2 %shard_map.55 = s32[1]{0:T(128)} custom-call(s32[4]{0:T(128)} %plan_ref.1, s32[4]{0:T(128)} %lives_ref.1), custom_call_target="tpu_custom_call" | custom-call | flops 40000000000 | tf_op jit(solution)/shard_map/pallas_call | solution.py:40
  20.6 9.9 %all-to-all-done.24 = bf16[8,8,2048]{2,1,0:T(8,128)(2,1)} async-done(((bf16[8,8,2048]{2,1,0:T(8,128)(2,1)}), bf16[8,8,2048]{2,1,0:T(8,128)(2,1)}, u32[]{:S(2)}, u32[]{:S(2)}) %all-to-all-start.24) | async-done | bytes 262176 | tf_op jit(solution)/shard_map/all_to_all | solution.py:131
  30.5 0.0 collective-permute-done.7
  30.5 64.3 %conditional.1 = (bf16[8,8,2048]{2,1,0:T(8,128)(2,1)S(1)}) conditional(s32[]{:T(128)} %bitcast.42, (s32[4]{0:T(128)S(1)}, s32[4]{0:T(128)S(1)}, bf16[8,8,2048]{2,1,0:T(8,128)(2,1)}, bf16[2,416,2048]{2,1,0:T(8,128)(2,1)S(1)}, bf16[2,416,2048]{2,1,0:T(8,128)(2,1)}, /*index=5*/bf16[416,2048]{1,0:T(8,128)(2,1)}, ...), branch_computations={%region_0.2_spmd, %region_2.4_spmd, %region_4.6_spmd, %region_6.8_... | conditional | flops 2625544192 | bytes 32719028 | solution.py:167
  30.6 1.1 branch_0_fun.3
  31.6 10.9 %all_to_all.106 = bf16[4,16,2048]{2,1,0:T(8,128)(2,1)S(1)} all-to-all(bf16[4,16,2048]{2,1,0:T(8,128)(2,1)S(1)} %bitcast.74), channel_id=1, replica_groups=mesh['zl'=8,'y'=4,'c'=2,'x'=4,'zh'=2] {'y'}, dimensions={0} | all-to-all | bytes 524288 | tf_op jit(solution)/shard_map/cond/branch_0_fun/all_to_all | solution.py:131
  42.6 4.2 %branch_0_fun.4 = f32[64,1664]{1,0:T(8,128)S(1)} custom-call(bf16[64,2048]{1,0:T(8,128)(2,1)S(1)} %bitcast.73, bf16[2,416,2048]{2,1,0:T(8,128)(2,1)S(1)} %get-tuple-element.98.own_ref, bf16[2,416,2048]{2,1,0:T(8,128)(2,1)} %get-tuple-element.100.other_ref), custom_call_target="tpu_custom_call" | custom-call | flops 436207616 | bytes 6815744 | tf_op jit(solution)/shard_map/cond/branch_0_fun/pallas_call | solution.py:107
  46.8 11.7 %all_to_all.107 = f32[4,16,1664]{2,1,0:T(8,128)S(1)} all-to-all(f32[4,16,1664]{2,1,0:T(8,128)S(1)} %bitcast.69), channel_id=1, replica_groups=mesh['zl'=8,'y'=4,'c'=2,'x'=4,'zh'=2] {'x'}, dimensions={0} | all-to-all | bytes 851968 | tf_op jit(solution)/shard_map/cond/branch_0_fun/all_to_all | solution.py:131
  58.5 8.2 %collective-permute-start = (bf16[16,1664]{1,0:T(8,128)(2,1)S(1)}, bf16[16,1664]{1,0:T(8,128)(2,1)S(1)}, u32[]{:S(2)}, u32[]{:S(2)}) collective-permute-start(bf16[16,1664]{1,0:T(8,128)(2,1)S(1)} %convert_element_type.78), channel_id=1, source_target_pairs={{0,1},{1,0},{2,3},{3,2},{4,5},{5,4},{6,7},{7,6},{8,9},{9,8},{10,11... | collective-permute-start | bytes 159752 | tf_op jit(solution)/shard_map/cond/branch_0_fun/ppermute | solution.py:135
  66.8 7.0 %collective-permute-done = bf16[16,1664]{1,0:T(8,128)(2,1)S(1)} collective-permute-done((bf16[16,1664]{1,0:T(8,128)(2,1)S(1)}, bf16[16,1664]{1,0:T(8,128)(2,1)S(1)}, u32[]{:S(2)}, u32[]{:S(2)}) %collective-permute-start) | collective-permute-done | bytes 53280 | tf_op jit(solution)/shard_map/cond/branch_0_fun/ppermute | solution.py:135
  73.7 0.1 fusion.7
  73.8 8.3 %all_to_all.108 = bf16[4,16,832]{2,1,0:T(8,128)(2,1)S(1)} all-to-all(bf16[4,16,832]{2,1,0:T(8,128)(2,1)S(1)} %broadcast_in_dim.3), channel_id=1, replica_groups=mesh['zl'=8,'y'=4,'c'=2,'x'=4,'zh'=2] {'x'}, dimensions={0} | all-to-all | bytes 212992 | tf_op jit(solution)/shard_map/cond/branch_0_fun/all_to_all | solution.py:131
  82.1 2.7 %fusion.4 = bf16[64,2048]{1,0:T(8,128)(2,1)S(1)} fusion(bf16[64,832]{1,0:T(8,128)(2,1)S(1)} %bitcast.94, bf16[416,2048]{1,0:T(8,128)(2,1)} %get-tuple-element.102, bf16[416,2048]{1,0:T(8,128)(2,1)} %get-tuple-element.101), kind=kOutput, calls=%fused_computation.4 | convolution fusion | flops 225050624 | bytes 3776512 | tf_op jit(solution)/shard_map/cond/branch_0_fun/dot_general | solution.py:157
  84.8 9.1 %all_to_all.109 = bf16[4,16,2048]{2,1,0:T(8,128)(2,1)S(1)} all-to-all(bf16[4,16,2048]{2,1,0:T(8,128)(2,1)S(1)} %bitcast.91), channel_id=1, replica_groups=mesh['zl'=8,'y'=4,'c'=2,'x'=4,'zh'=2] {'y'}, dimensions={0} | all-to-all | bytes 524288 | tf_op jit(solution)/shard_map/cond/branch_0_fun/all_to_all | solution.py:131
  93.9 0.7 branch_0_fun.5
  94.9 17.5 %all_to_all.130 = bf16[8,8,2048]{2,1,0:T(8,128)(2,1)S(1)} all-to-all(bf16[8,8,2048]{2,1,0:T(8,128)(2,1)S(1)} %get-tuple-element.138), channel_id=1, replica_groups=mesh['zl'=8,'y'=4,'c'=2,'x'=4,'zh'=2] {'zl'}, dimensions={0} | all-to-all | bytes 524288 | tf_op jit(solution)/shard_map/all_to_all | solution.py:131
  112.4 0.7 fusion.54
  (8 shorter events, 0.1 us)
Async XLA Ops:
  1.5 29.0 %all-to-all-start.24 = ((bf16[8,8,2048]{2,1,0:T(8,128)(2,1)}), bf16[8,8,2048]{2,1,0:T(8,128)(2,1)}, u32[]{:S(2)}, u32[]{:S(2)}) async-start(bf16[8,8,2048]{2,1,0:T(8,128)(2,1)} %broadcast_in_dim.22), calls=%async_computation.24 | async-start | bytes 524288 | tf_op jit(solution)/shard_map/all_to_all | solution.py:131
  14.1 16.4 %collective-permute-start.7 = (bf16[416,2048]{1,0:T(8,128)(2,1)}, bf16[416,2048]{1,0:T(8,128)(2,1)}, u32[]{:S(2)}, u32[]{:S(2)}) collective-permute-start(bf16[416,2048]{1,0:T(8,128)(2,1)} %param.15), channel_id=1, source_target_pairs={{0,8},{8,0},{1,9},{9,1},{2,10},{10,2},{3,11},{11,3},{4,12},{12,4},... | collective-permute-start | bytes 5111816 | tf_op jit(solution)/shard_map/ppermute | solution.py:135
  16.1 14.5 %copy-start = (bf16[2048,2,416]{0,2,1:T(8,128)(2,1)S(1)}, bf16[2048,2,416]{0,2,1:T(8,128)(2,1)}, u32[]{:S(2)}) copy-start(bf16[2048,2,416]{0,2,1:T(8,128)(2,1)} %param.14) | copy-start | bytes 10223620
  16.1 14.5 %copy-start.1 = (s32[4]{0:T(128)S(1)}, s32[4]{0:T(128)}, u32[]{:S(2)}) copy-start(s32[4]{0:T(128)} %plan_ref.1) | copy-start | bytes 52
  16.1 14.5 %copy-start.2 = (s32[4]{0:T(128)S(1)}, s32[4]{0:T(128)}, u32[]{:S(2)}) copy-start(s32[4]{0:T(128)} %lives_ref.1) | copy-start | bytes 52
  16.1 14.4 %collective-permute-start.6 = (bf16[2,416,2048]{2,1,0:T(8,128)(2,1)}, bf16[2,416,2048]{2,1,0:T(8,128)(2,1)}, u32[]{:S(2)}, u32[]{:S(2)}) collective-permute-start(bf16[2,416,2048]{2,1,0:T(8,128)(2,1)} %bitcast.76), channel_id=1, source_target_pairs={{0,8},{8,0},{1,9},{9,1},{2,10},{10,2},{3,11},{11,3},{4,12},{12,4},... | collective-permute-start | bytes 10223624 | tf_op jit(solution)/shard_map/ppermute | solution.py:135
  58.5 15.2 %collective-permute-start = (bf16[16,1664]{1,0:T(8,128)(2,1)S(1)}, bf16[16,1664]{1,0:T(8,128)(2,1)S(1)}, u32[]{:S(2)}, u32[]{:S(2)}) collective-permute-start(bf16[16,1664]{1,0:T(8,128)(2,1)S(1)} %convert_element_type.78), channel_id=1, source_target_pairs={{0,1},{1,0},{2,3},{3,2},{4,5},{5,4},{6,7},{7,6},{8,9},{9,8},{10,11... | collective-permute-start | bytes 159752 | tf_op jit(solution)/shard_map/cond/branch_0_fun/ppermute | solution.py:135

commit v2 on v1

--- a/solution.py
+++ b/solution.py
@@ -12,6 +12,7 @@
 HALF = 64
 ZL, YY, CC, XX, ZH = 8, 4, 2, 4, 2
 HIDE = 40_000_000_000
+GATHER = (5, 6)
 WIDE = 256
 SIZES = (2, 3, 4, 5, 6, 8)
 BF16, F32 = jnp.bfloat16, jnp.float32
@@ -57,14 +58,14 @@
         def _():
             kept = row + HALF * part < lives_ref[block]
             rows = jnp.where(kept, rows_ref[h].astype(F32), 0.0).astype(BF16)
-            for copy in range(YY):
+            for copy in range(out_ref.shape[0]):
                 out_ref[copy, slot] = rows
 
     for s in range(slots):
 
         @pl.when(s >= count)
         def _():
-            for copy in range(YY):
+            for copy in range(out_ref.shape[0]):
                 out_ref[copy, s] = jnp.zeros(out_ref.shape[2:], BF16)
 
 
@@ -143,8 +144,12 @@
     features, hidden = own.shape[2], 2 * down[0].shape[0]
     per = slots * 8
     place = (lax.axis_index("y") * 16 + lax.axis_index("c") * 8).reshape(1)
-    packed = local_call(functools.partial(pack_kernel, slots), 3, (YY, slots, 8, features))(plan, lives, place, gathered)
-    rows = exchange(packed.reshape(YY, per, features), "y").reshape(YY * per, features)
+    copies = 1 if slots in GATHER else YY
+    packed = local_call(functools.partial(pack_kernel, slots), 3, (copies, slots, 8, features))(plan, lives, place, gathered)
+    if copies == 1:
+        rows = lax.all_gather(packed.reshape(per, features), "y", axis=0, tiled=True)
+    else:
+        rows = exchange(packed.reshape(YY, per, features), "y").reshape(YY * per, features)
 
     partial = project(rows, own, other)
     along_x = jnp.sum(exchange(partial.reshape(XX, per, 2 * hidden), "x"), axis=0)

time: 114 us -> 129 us (1.13)
  blocking collectives: 57.5 us -> 67.7 us
  waiting for transfers between devices: 16.8 us -> 22 us
    all_gather x0 -> x1, blocking collectives: none -> 13.7 us  [block_rows(): lax.all_gather(packed.reshape(per, features), 'y', axis=0, tiled=True)]
    ppermute x3, waiting for transfers between devices: 6.96 us -> 12.1 us  [swap(): return lax.ppermute(array, axis, [(0, 1), (1, 0)])]
    all_to_all x5 -> x4, blocking collectives: 57.5 us -> 54 us  [exchange(): return lax.all_to_all(array, axis, 0, 0, tiled=False)]
where the time goes in v2:
time: 129 us
  blocking collectives  67.7 us (52%)
  starting transfers between devices  25.4 us (20%)
  waiting for transfers between devices  22 us (17%)
  Pallas kernels  7.46 us (6%)
  matrix products  2.33 us (2%)
  local copies, waits for them, and re-layouts  1.55 us (1%)
    all_to_all x4, blocking collectives, exchange(): return lax.all_to_all(array, axis, 0, 0, tiled=False)  54 us
    all_gather x1, blocking collectives, block_rows(): lax.all_gather(packed.reshape(per, features), 'y', axis=0, tiled=True)  13.7 us
    ppermute x3, starting transfers between devices, swap(): return lax.ppermute(array, axis, [(0, 1), (1, 0)])  12.8 us
    all_to_all x1, starting transfers between devices, exchange(): return lax.all_to_all(array, axis, 0, 0, tiled=False)  12.6 us
    ppermute x3, waiting for transfers between devices, swap(): return lax.ppermute(array, axis, [(0, 1), (1, 0)])  12.1 us
    all_to_all x1, waiting for transfers between devices, exchange(): return lax.all_to_all(array, axis, 0, 0, tiled=False)  9.88 us
    pallas_call x1, Pallas kernels, project(): pl.pallas_call(project_kernel, out_shape=jax.ShapeDtypeStruct((count, col...  4.46 us
  transfers between devices with their start and end apart: 4, of which 2 were waited for; matrix products, arithmetic and copies ran while one was open for 0% of the time, Pallas kernels for 1%

profile of v2, /device:TPU:32, one launch (start us, length us, event | category | flops | bytes accessed | tf_op | source)
XLA Modules:
  0.0 128.6 jit_solution(13844394873889749437)
XLA Ops:
  0.0 1.5 %broadcast_in_dim.22 = bf16[8,8,2048]{2,1,0:T(8,128)(2,1)} broadcast(bf16[8,2048]{1,0:T(8,128)(2,1)} %param.11), dimensions={1,2} | broadcast | bytes 294912 | tf_op jit(solution)/shard_map/broadcast_in_dim | solution.py:140
  1.5 12.6 %all-to-all-start.22 = ((bf16[8,8,2048]{2,1,0:T(8,128)(2,1)}), bf16[8,8,2048]{2,1,0:T(8,128)(2,1)}, u32[]{:S(2)}, u32[]{:S(2)}) async-start(bf16[8,8,2048]{2,1,0:T(8,128)(2,1)} %broadcast_in_dim.22), calls=%async_computation.22 | async-start | bytes 524288 | tf_op jit(solution)/shard_map/all_to_all | solution.py:132
  14.1 1.9 %collective-permute-start.7 = (bf16[416,2048]{1,0:T(8,128)(2,1)}, bf16[416,2048]{1,0:T(8,128)(2,1)}, u32[]{:S(2)}, u32[]{:S(2)}) collective-permute-start(bf16[416,2048]{1,0:T(8,128)(2,1)} %param.15), channel_id=1, source_target_pairs={{0,8},{8,0},{1,9},{9,1},{2,10},{10,2},{3,11},{11,3},{4,12},{12,4},... | collective-permute-start | bytes 5111816 | tf_op jit(solution)/shard_map/ppermute | solution.py:136
  16.1 0.0 copy-start
  16.1 0.0 copy-start.1
  16.1 0.0 copy-start.2
  16.1 2.7 %collective-permute-start.6 = (bf16[2,416,2048]{2,1,0:T(8,128)(2,1)}, bf16[2,416,2048]{2,1,0:T(8,128)(2,1)}, u32[]{:S(2)}, u32[]{:S(2)}) collective-permute-start(bf16[2,416,2048]{2,1,0:T(8,128)(2,1)} %bitcast.72), channel_id=1, source_target_pairs={{0,8},{8,0},{1,9},{9,1},{2,10},{10,2},{3,11},{11,3},{4,12},{12,4},... | collective-permute-start | bytes 10223624 | tf_op jit(solution)/shard_map/ppermute | solution.py:136
  18.8 1.2 shard_map.55
  20.6 9.9 %all-to-all-done.22 = bf16[8,8,2048]{2,1,0:T(8,128)(2,1)} async-done(((bf16[8,8,2048]{2,1,0:T(8,128)(2,1)}), bf16[8,8,2048]{2,1,0:T(8,128)(2,1)}, u32[]{:S(2)}, u32[]{:S(2)}) %all-to-all-start.22) | async-done | bytes 262176 | tf_op jit(solution)/shard_map/all_to_all | solution.py:132
  30.5 80.4 %conditional.1 = (bf16[8,8,2048]{2,1,0:T(8,128)(2,1)S(1)}) conditional(s32[]{:T(128)} %bitcast.40, (s32[4]{0:T(128)S(1)}, s32[4]{0:T(128)S(1)}, bf16[8,8,2048]{2,1,0:T(8,128)(2,1)}, bf16[2,416,2048]{2,1,0:T(8,128)(2,1)S(1)}, bf16[2,416,2048]{2,1,0:T(8,128)(2,1)}, /*index=5*/bf16[416,2048]{1,0:T(8,128)(2,1)}, ...), branch_computations={%region_0.2_spmd, %region_2.4_spmd, %region_4.6_spmd, %region_6.8_... | conditional | flops 2625544192 | bytes 32719028 | solution.py:172
  30.6 1.1 branch_3_fun.3
  31.7 13.7 %all_gather.4.rows_ref = bf16[160,2048]{1,0:T(8,128)(2,1)S(1)} all-gather(bf16[40,2048]{1,0:T(8,128)(2,1)S(1)} %bitcast.71), channel_id=1, replica_groups=mesh['zl'=8,'y'=4,'c'=2,'x'=4,'zh'=2] {'y'}, dimensions={0}, use_global_device_ids=true | all-gather | bytes 819200 | tf_op jit(solution)/shard_map/cond/branch_3_fun/all_gather | solution.py:150
  45.4 4.5 %branch_3_fun.4 = f32[160,1664]{1,0:T(8,128)S(1)} custom-call(bf16[160,2048]{1,0:T(8,128)(2,1)S(1)} %all_gather.4.rows_ref, bf16[2,416,2048]{2,1,0:T(8,128)(2,1)S(1)} %get-tuple-element.120.own_ref, bf16[2,416,2048]{2,1,0:T(8,128)(2,1)} %get-tuple-element.121.other_ref), custom_call_target="tpu_custom_call" | custom-call | flops 1090519040 | bytes 6815744 | tf_op jit(solution)/shard_map/cond/branch_3_fun/pallas_call | solution.py:108
  49.9 15.2 %all_to_all.110 = f32[4,40,1664]{2,1,0:T(8,128)S(1)} all-to-all(f32[4,40,1664]{2,1,0:T(8,128)S(1)} %bitcast.52), channel_id=1, replica_groups=mesh['zl'=8,'y'=4,'c'=2,'x'=4,'zh'=2] {'x'}, dimensions={0} | all-to-all | bytes 2129920 | tf_op jit(solution)/shard_map/cond/branch_3_fun/all_to_all | solution.py:132
  65.1 0.1 reduce_sum.51
  65.2 8.2 %collective-permute-start.3 = (bf16[40,1664]{1,0:T(8,128)(2,1)S(1)}, bf16[40,1664]{1,0:T(8,128)(2,1)S(1)}, u32[]{:S(2)}, u32[]{:S(2)}) collective-permute-start(bf16[40,1664]{1,0:T(8,128)(2,1)S(1)} %convert_element_type.90), channel_id=1, source_target_pairs={{0,1},{1,0},{2,3},{3,2},{4,5},{5,4},{6,7},{7,6},{8,9},{9,8},{10,11... | collective-permute-start | bytes 399368 | tf_op jit(solution)/shard_map/cond/branch_3_fun/ppermute | solution.py:136
  73.4 12.1 %collective-permute-done.3 = bf16[40,1664]{1,0:T(8,128)(2,1)S(1)} collective-permute-done((bf16[40,1664]{1,0:T(8,128)(2,1)S(1)}, bf16[40,1664]{1,0:T(8,128)(2,1)S(1)}, u32[]{:S(2)}, u32[]{:S(2)}) %collective-permute-start.3) | collective-permute-done | bytes 133152 | tf_op jit(solution)/shard_map/cond/branch_3_fun/ppermute | solution.py:136
  85.5 0.1 fusion.34
  85.7 9.2 %all_to_all.111 = bf16[4,40,832]{2,1,0:T(8,128)(2,1)S(1)} all-to-all(bf16[4,40,832]{2,1,0:T(8,128)(2,1)S(1)} %broadcast_in_dim.14), channel_id=1, replica_groups=mesh['zl'=8,'y'=4,'c'=2,'x'=4,'zh'=2] {'x'}, dimensions={0} | all-to-all | bytes 532480 | tf_op jit(solution)/shard_map/cond/branch_3_fun/all_to_all | solution.py:132
  94.9 2.3 %fusion.31 = bf16[160,2048]{1,0:T(8,128)(2,1)S(1)} fusion(bf16[160,832]{1,0:T(8,128)(2,1)S(1)} %bitcast.86, bf16[416,2048]{1,0:T(8,128)(2,1)} %get-tuple-element.123, bf16[416,2048]{1,0:T(8,128)(2,1)S(1)} %copy-done.5), kind=kOutput, calls=%fused_computation.31 | convolution fusion | flops 552402944 | bytes 4329472 | tf_op jit(solution)/shard_map/cond/branch_3_fun/dot_general | solution.py:162
  97.2 12.6 %all_to_all.112 = bf16[4,40,2048]{2,1,0:T(8,128)(2,1)S(1)} all-to-all(bf16[4,40,2048]{2,1,0:T(8,128)(2,1)S(1)} %bitcast.81), channel_id=1, replica_groups=mesh['zl'=8,'y'=4,'c'=2,'x'=4,'zh'=2] {'y'}, dimensions={0} | all-to-all | bytes 1310720 | tf_op jit(solution)/shard_map/cond/branch_3_fun/all_to_all | solution.py:132
  109.8 0.7 branch_3_fun.5
  111.0 17.0 %all_to_all.120 = bf16[8,8,2048]{2,1,0:T(8,128)(2,1)S(1)} all-to-all(bf16[8,8,2048]{2,1,0:T(8,128)(2,1)S(1)} %get-tuple-element.138), channel_id=1, replica_groups=mesh['zl'=8,'y'=4,'c'=2,'x'=4,'zh'=2] {'zl'}, dimensions={0} | all-to-all | bytes 524288 | tf_op jit(solution)/shard_map/all_to_all | solution.py:132
  128.0 0.7 fusion.54
  (10 shorter events, 0.1 us)
Async XLA Ops:
  1.5 29.0 %all-to-all-start.22 = ((bf16[8,8,2048]{2,1,0:T(8,128)(2,1)}), bf16[8,8,2048]{2,1,0:T(8,128)(2,1)}, u32[]{:S(2)}, u32[]{:S(2)}) async-start(bf16[8,8,2048]{2,1,0:T(8,128)(2,1)} %broadcast_in_dim.22), calls=%async_computation.22 | async-start | bytes 524288 | tf_op jit(solution)/shard_map/all_to_all | solution.py:132
  14.1 16.4 %collective-permute-start.7 = (bf16[416,2048]{1,0:T(8,128)(2,1)}, bf16[416,2048]{1,0:T(8,128)(2,1)}, u32[]{:S(2)}, u32[]{:S(2)}) collective-permute-start(bf16[416,2048]{1,0:T(8,128)(2,1)} %param.15), channel_id=1, source_target_pairs={{0,8},{8,0},{1,9},{9,1},{2,10},{10,2},{3,11},{11,3},{4,12},{12,4},... | collective-permute-start | bytes 5111816 | tf_op jit(solution)/shard_map/ppermute | solution.py:136
  16.1 14.5 %copy-start = (bf16[2048,2,416]{0,2,1:T(8,128)(2,1)S(1)}, bf16[2048,2,416]{0,2,1:T(8,128)(2,1)}, u32[]{:S(2)}) copy-start(bf16[2048,2,416]{0,2,1:T(8,128)(2,1)} %param.14) | copy-start | bytes 10223620
  16.1 14.5 %copy-start.1 = (s32[4]{0:T(128)S(1)}, s32[4]{0:T(128)}, u32[]{:S(2)}) copy-start(s32[4]{0:T(128)} %plan_ref.1) | copy-start | bytes 52
  16.1 14.5 %copy-start.2 = (s32[4]{0:T(128)S(1)}, s32[4]{0:T(128)}, u32[]{:S(2)}) copy-start(s32[4]{0:T(128)} %lives_ref.1) | copy-start | bytes 52
  16.1 14.4 %collective-permute-start.6 = (bf16[2,416,2048]{2,1,0:T(8,128)(2,1)}, bf16[2,416,2048]{2,1,0:T(8,128)(2,1)}, u32[]{:S(2)}, u32[]{:S(2)}) collective-permute-start(bf16[2,416,2048]{2,1,0:T(8,128)(2,1)} %bitcast.72), channel_id=1, source_target_pairs={{0,8},{8,0},{1,9},{9,1},{2,10},{10,2},{3,11},{11,3},{4,12},{12,4},... | collective-permute-start | bytes 10223624 | tf_op jit(solution)/shard_map/ppermute | solution.py:136
  49.9 45.0 %copy-start.5 = (bf16[416,2048]{1,0:T(8,128)(2,1)S(1)}, bf16[416,2048]{1,0:T(8,128)(2,1)}, u32[]{:S(2)}) copy-start(bf16[416,2048]{1,0:T(8,128)(2,1)} %get-tuple-element.122) | copy-start | bytes 5111812 | tf_op jit(solution)/shard_map/cond
  65.2 20.3 %collective-permute-start.3 = (bf16[40,1664]{1,0:T(8,128)(2,1)S(1)}, bf16[40,1664]{1,0:T(8,128)(2,1)S(1)}, u32[]{:S(2)}, u32[]{:S(2)}) collective-permute-start(bf16[40,1664]{1,0:T(8,128)(2,1)S(1)} %convert_element_type.90), channel_id=1, source_target_pairs={{0,1},{1,0},{2,3},{3,2},{4,5},{5,4},{6,7},{7,6},{8,9},{9,8},{10,11... | collective-permute-start | bytes 399368 | tf_op jit(solution)/shard_map/cond/branch_3_fun/ppermute | solution.py:136

commit v3 on v2

--- a/solution.py
+++ b/solution.py
@@ -14,7 +14,7 @@
 HIDE = 40_000_000_000
 GATHER = (5, 6)
 WIDE = 256
-SIZES = (2, 3, 4, 5, 6, 8)
+SIZES = (1, 2, 3, 4, 5, 6, 7, 8)
 BF16, F32 = jnp.bfloat16, jnp.float32
 
 

time: 129 us -> 132 us (1.023); the launches traced: 129 us -> 134 us
  waiting for transfers between devices: 22 us -> 25.3 us
  blocking collectives: 67.7 us -> 69.3 us
    ppermute x3, waiting for transfers between devices: 12.1 us -> 15.4 us  [swap(): return lax.ppermute(array, axis, [(0, 1), (1, 0)])]
    all_to_all x4, blocking collectives: 54 us -> 55.4 us  [exchange(): return lax.all_to_all(array, axis, 0, 0, tiled=False)]
where the time goes in v3:
time: 132 us; the launch traced here: 134 us
  blocking collectives  69.3 us (52%)
  starting transfers between devices  25.4 us (19%)
  waiting for transfers between devices  25.3 us (19%)
  Pallas kernels  7.61 us (6%)
  matrix products  3 us (2%)
  local copies, waits for them, and re-layouts  1.53 us (1%)
    all_to_all x4, blocking collectives, exchange(): return lax.all_to_all(array, axis, 0, 0, tiled=False)  55.4 us
    ppermute x3, waiting for transfers between devices, swap(): return lax.ppermute(array, axis, [(0, 1), (1, 0)])  15.4 us
    all_gather x1, blocking collectives, block_rows(): lax.all_gather(packed.reshape(per, features), 'y', axis=0, tiled=True)  13.9 us
    ppermute x3, starting transfers between devices, swap(): return lax.ppermute(array, axis, [(0, 1), (1, 0)])  12.8 us
    all_to_all x1, starting transfers between devices, exchange(): return lax.all_to_all(array, axis, 0, 0, tiled=False)  12.6 us
    all_to_all x1, waiting for transfers between devices, exchange(): return lax.all_to_all(array, axis, 0, 0, tiled=False)  9.88 us
    pallas_call x1, Pallas kernels, project(): pl.pallas_call(project_kernel, out_shape=jax.ShapeDtypeStruct((count, col...  4.58 us
    dot_general x1, matrix products, block_rows(): ours = jnp.dot(act, down, preferred_element_type=F32).astype(BF16)  3 us
  transfers between devices with their start and end apart: 4, of which 2 were waited for; matrix products, arithmetic and copies ran while one was open for 0% of the time, Pallas kernels for 1%

profile of v3, /device:TPU:32, one launch (start us, length us, event | category | flops | bytes accessed | tf_op | source)
XLA Modules:
  0.0 134.4 jit_solution(18316830296004934920)
XLA Ops:
  0.0 1.5 %broadcast_in_dim.30 = bf16[8,8,2048]{2,1,0:T(8,128)(2,1)} broadcast(bf16[8,2048]{1,0:T(8,128)(2,1)} %param.13), dimensions={1,2} | broadcast | bytes 294912 | tf_op jit(solution)/shard_map/broadcast_in_dim | solution.py:140
  1.5 12.6 %all-to-all-start.30 = ((bf16[8,8,2048]{2,1,0:T(8,128)(2,1)}), bf16[8,8,2048]{2,1,0:T(8,128)(2,1)}, u32[]{:S(2)}, u32[]{:S(2)}) async-start(bf16[8,8,2048]{2,1,0:T(8,128)(2,1)} %broadcast_in_dim.30), calls=%async_computation.30 | async-start | bytes 524288 | tf_op jit(solution)/shard_map/all_to_all | solution.py:132
  14.1 1.9 %collective-permute-start.9 = (bf16[416,2048]{1,0:T(8,128)(2,1)}, bf16[416,2048]{1,0:T(8,128)(2,1)}, u32[]{:S(2)}, u32[]{:S(2)}) collective-permute-start(bf16[416,2048]{1,0:T(8,128)(2,1)} %param.17), channel_id=1, source_target_pairs={{0,8},{8,0},{1,9},{9,1},{2,10},{10,2},{3,11},{11,3},{4,12},{12,4},... | collective-permute-start | bytes 5111816 | tf_op jit(solution)/shard_map/ppermute | solution.py:136
  16.0 0.0 copy-start
  16.1 0.0 copy-start.1
  16.1 0.0 copy-start.2
  16.1 2.7 %collective-permute-start.8 = (bf16[2,416,2048]{2,1,0:T(8,128)(2,1)}, bf16[2,416,2048]{2,1,0:T(8,128)(2,1)}, u32[]{:S(2)}, u32[]{:S(2)}) collective-permute-start(bf16[2,416,2048]{2,1,0:T(8,128)(2,1)} %bitcast.98), channel_id=1, source_target_pairs={{0,8},{8,0},{1,9},{9,1},{2,10},{10,2},{3,11},{11,3},{4,12},{12,4},... | collective-permute-start | bytes 10223624 | tf_op jit(solution)/shard_map/ppermute | solution.py:136
  18.8 1.2 shard_map.55
  20.6 9.9 %all-to-all-done.30 = bf16[8,8,2048]{2,1,0:T(8,128)(2,1)} async-done(((bf16[8,8,2048]{2,1,0:T(8,128)(2,1)}), bf16[8,8,2048]{2,1,0:T(8,128)(2,1)}, u32[]{:S(2)}, u32[]{:S(2)}) %all-to-all-start.30) | async-done | bytes 262176 | tf_op jit(solution)/shard_map/all_to_all | solution.py:132
  30.5 86.3 %conditional.1 = (bf16[8,8,2048]{2,1,0:T(8,128)(2,1)S(1)}) conditional(s32[]{:T(128)} %bitcast.54, (s32[4]{0:T(128)S(1)}, s32[4]{0:T(128)S(1)}, bf16[8,8,2048]{2,1,0:T(8,128)(2,1)}, bf16[2,416,2048]{2,1,0:T(8,128)(2,1)S(1)}, bf16[2,416,2048]{2,1,0:T(8,128)(2,1)}, /*index=5*/bf16[416,2048]{1,0:T(8,128)(2,1)}, ...), branch_computations={%region_0.2_spmd, %region_2.4_spmd, %region_4.6_spmd, %region_6.8_... | conditional | flops 2625544192 | bytes 32719028 | solution.py:172
  30.8 1.1 branch_5_fun.3
  31.9 13.9 %all_gather.5.rows_ref = bf16[192,2048]{1,0:T(8,128)(2,1)S(1)} all-gather(bf16[48,2048]{1,0:T(8,128)(2,1)S(1)} %bitcast.93), channel_id=1, replica_groups=mesh['zl'=8,'y'=4,'c'=2,'x'=4,'zh'=2] {'y'}, dimensions={0}, use_global_device_ids=true | all-gather | bytes 983040 | tf_op jit(solution)/shard_map/cond/branch_5_fun/all_gather | solution.py:150
  45.8 4.6 %branch_5_fun.4 = f32[192,1664]{1,0:T(8,128)S(1)} custom-call(bf16[192,2048]{1,0:T(8,128)(2,1)S(1)} %all_gather.5.rows_ref, bf16[2,416,2048]{2,1,0:T(8,128)(2,1)S(1)} %get-tuple-element.164.own_ref, bf16[2,416,2048]{2,1,0:T(8,128)(2,1)} %get-tuple-element.165.other_ref), custom_call_target="tpu_custom_call" | custom-call | flops 1308622848 | bytes 6815744 | tf_op jit(solution)/shard_map/cond/branch_5_fun/pallas_call | solution.py:108
  50.4 16.2 %all_to_all.149 = f32[4,48,1664]{2,1,0:T(8,128)S(1)} all-to-all(f32[4,48,1664]{2,1,0:T(8,128)S(1)} %bitcast.70), channel_id=1, replica_groups=mesh['zl'=8,'y'=4,'c'=2,'x'=4,'zh'=2] {'x'}, dimensions={0} | all-to-all | bytes 2555904 | tf_op jit(solution)/shard_map/cond/branch_5_fun/all_to_all | solution.py:132
  66.6 0.1 reduce_sum.69
  66.7 8.2 %collective-permute-start.5 = (bf16[48,1664]{1,0:T(8,128)(2,1)S(1)}, bf16[48,1664]{1,0:T(8,128)(2,1)S(1)}, u32[]{:S(2)}, u32[]{:S(2)}) collective-permute-start(bf16[48,1664]{1,0:T(8,128)(2,1)S(1)} %convert_element_type.114), channel_id=1, source_target_pairs={{0,1},{1,0},{2,3},{3,2},{4,5},{5,4},{6,7},{7,6},{8,9},{9,8},{10,11... | collective-permute-start | bytes 479240 | tf_op jit(solution)/shard_map/cond/branch_5_fun/ppermute | solution.py:136
  74.9 15.4 %collective-permute-done.5 = bf16[48,1664]{1,0:T(8,128)(2,1)S(1)} collective-permute-done((bf16[48,1664]{1,0:T(8,128)(2,1)S(1)}, bf16[48,1664]{1,0:T(8,128)(2,1)S(1)}, u32[]{:S(2)}, u32[]{:S(2)}) %collective-permute-start.5) | collective-permute-done | bytes 159776 | tf_op jit(solution)/shard_map/cond/branch_5_fun/ppermute | solution.py:136
  90.4 0.1 fusion.56
  90.5 9.5 %all_to_all.150 = bf16[4,48,832]{2,1,0:T(8,128)(2,1)S(1)} all-to-all(bf16[4,48,832]{2,1,0:T(8,128)(2,1)S(1)} %broadcast_in_dim.22), channel_id=1, replica_groups=mesh['zl'=8,'y'=4,'c'=2,'x'=4,'zh'=2] {'x'}, dimensions={0} | all-to-all | bytes 638976 | tf_op jit(solution)/shard_map/cond/branch_5_fun/all_to_all | solution.py:132
  100.0 3.0 %fusion.53 = bf16[192,2048]{1,0:T(8,128)(2,1)S(1)} fusion(bf16[192,832]{1,0:T(8,128)(2,1)S(1)} %bitcast.115, bf16[416,2048]{1,0:T(8,128)(2,1)} %get-tuple-element.167, bf16[416,2048]{1,0:T(8,128)(2,1)} %get-tuple-element.166), kind=kOutput, calls=%fused_computation.51 | convolution fusion | flops 661520384 | bytes 4513792 | tf_op jit(solution)/shard_map/cond/branch_5_fun/dot_general | solution.py:162
  103.0 12.8 %all_to_all.151 = bf16[4,48,2048]{2,1,0:T(8,128)(2,1)S(1)} all-to-all(bf16[4,48,2048]{2,1,0:T(8,128)(2,1)S(1)} %bitcast.109), channel_id=1, replica_groups=mesh['zl'=8,'y'=4,'c'=2,'x'=4,'zh'=2] {'y'}, dimensions={0} | all-to-all | bytes 1572864 | tf_op jit(solution)/shard_map/cond/branch_5_fun/all_to_all | solution.py:132
  115.8 0.7 branch_5_fun.5
  116.8 16.9 %all_to_all.160 = bf16[8,8,2048]{2,1,0:T(8,128)(2,1)S(1)} all-to-all(bf16[8,8,2048]{2,1,0:T(8,128)(2,1)S(1)} %get-tuple-element.182), channel_id=1, replica_groups=mesh['zl'=8,'y'=4,'c'=2,'x'=4,'zh'=2] {'zl'}, dimensions={0} | all-to-all | bytes 524288 | tf_op jit(solution)/shard_map/all_to_all | solution.py:132
  133.8 0.7 fusion.76
  (8 shorter events, 0.1 us)
Async XLA Ops:
  1.5 29.0 %all-to-all-start.30 = ((bf16[8,8,2048]{2,1,0:T(8,128)(2,1)}), bf16[8,8,2048]{2,1,0:T(8,128)(2,1)}, u32[]{:S(2)}, u32[]{:S(2)}) async-start(bf16[8,8,2048]{2,1,0:T(8,128)(2,1)} %broadcast_in_dim.30), calls=%async_computation.30 | async-start | bytes 524288 | tf_op jit(solution)/shard_map/all_to_all | solution.py:132
  14.1 16.4 %collective-permute-start.9 = (bf16[416,2048]{1,0:T(8,128)(2,1)}, bf16[416,2048]{1,0:T(8,128)(2,1)}, u32[]{:S(2)}, u32[]{:S(2)}) collective-permute-start(bf16[416,2048]{1,0:T(8,128)(2,1)} %param.17), channel_id=1, source_target_pairs={{0,8},{8,0},{1,9},{9,1},{2,10},{10,2},{3,11},{11,3},{4,12},{12,4},... | collective-permute-start | bytes 5111816 | tf_op jit(solution)/shard_map/ppermute | solution.py:136
  16.0 14.5 %copy-start = (bf16[2048,2,416]{0,2,1:T(8,128)(2,1)S(1)}, bf16[2048,2,416]{0,2,1:T(8,128)(2,1)}, u32[]{:S(2)}) copy-start(bf16[2048,2,416]{0,2,1:T(8,128)(2,1)} %param.16) | copy-start | bytes 10223620
  16.1 14.5 %copy-start.1 = (s32[4]{0:T(128)S(1)}, s32[4]{0:T(128)}, u32[]{:S(2)}) copy-start(s32[4]{0:T(128)} %plan_ref.1) | copy-start | bytes 52
  16.1 14.5 %copy-start.2 = (s32[4]{0:T(128)S(1)}, s32[4]{0:T(128)}, u32[]{:S(2)}) copy-start(s32[4]{0:T(128)} %lives_ref.1) | copy-start | bytes 52
  16.1 14.4 %collective-permute-start.8 = (bf16[2,416,2048]{2,1,0:T(8,128)(2,1)}, bf16[2,416,2048]{2,1,0:T(8,128)(2,1)}, u32[]{:S(2)}, u32[]{:S(2)}) collective-permute-start(bf16[2,416,2048]{2,1,0:T(8,128)(2,1)} %bitcast.98), channel_id=1, source_target_pairs={{0,8},{8,0},{1,9},{9,1},{2,10},{10,2},{3,11},{11,3},{4,12},{12,4},... | collective-permute-start | bytes 10223624 | tf_op jit(solution)/shard_map/ppermute | solution.py:136
  66.7 23.6 %collective-permute-start.5 = (bf16[48,1664]{1,0:T(8,128)(2,1)S(1)}, bf16[48,1664]{1,0:T(8,128)(2,1)S(1)}, u32[]{:S(2)}, u32[]{:S(2)}) collective-permute-start(bf16[48,1664]{1,0:T(8,128)(2,1)S(1)} %convert_element_type.114), channel_id=1, source_target_pairs={{0,1},{1,0},{2,3},{3,2},{4,5},{5,4},{6,7},{7,6},{8,9},{9,8},{10,11... | collective-permute-start | bytes 479240 | tf_op jit(solution)/shard_map/cond/branch_5_fun/ppermute | solution.py:136
